TPU v7x, 32 devices: a whole 2x2x4 slice. The times are simulated.
32 devices in a mesh: row: 4 (over y, core), col: 8 (over z, x).
Axes of the slice: x: 2, y: 2, z: 4, core: 2. Of those that a mesh axis runs over, the one named last changes fastest.
Arguments:
- features: bfloat16 [4096, 128], P(('row', 'col')), may hold values from -6 to 6
- norm_weight: float32 [4096], P(('row', 'col')), may hold values from 0.01767767 to 0.110485435
- weight_in: bfloat16 [128, 256], replicated, may hold values from -6 to 6
- weight_out: bfloat16 [256, 128], replicated, may hold values from -6 to 6
- labels: int32 [4096], P(('row', 'col')), may hold values from 0 to 127
- tile_slot: int32 [32, 128], P(('row', 'col')), may hold values from 0 to 31
- tile_edges: int32 [32, 128, 2, 512], P(('row', 'col')), may hold values from 0 to 127
- tile_count: int32 [32], P(('row', 'col')), may hold values from 32 to 128, as said below
Outputs:
- grad_in: float32 [128, 256], replicated
- grad_out: float32 [256, 128], replicated
- loss: float32 [], replicated
Inputs may be any that keep to these rules, and one draw needn't show every extreme that they name: `tile_slot`: position p of a slot covers the tile whose target rows start at 128 * (p // 4) and whose source columns start at 128 * (p % 4) within the device's block; a position may occur in several slots. Entry k of a slot marks row tile_edges[s, 0, k] and column tile_edges[s, 1, k] of its slot's tile; repeated entries count again. `tile_count`: slots at and after this number are not live; in every draw some device has all 128 slots live and another device only 32.
All inputs are finite; a program needn't handle non-finite values.
Results may differ from a plain program's by a relative error of at most 0.0084.
Values may be sent and summed in bfloat16 or wider, within the bound.
A program may use at most 64 MiB of HBM per device.

v0:
```python
import jax
import jax.numpy as jnp
from jax import lax
from jax.sharding import PartitionSpec as P

TILE = 128
SOFTCAP = 15.0
LOSS_SCALE = 1024.0
HIGHEST = lax.Precision.HIGHEST
CONTRACT_ROWS = (((0,), (0,)), ((), ()))


def densify(tile_slot, tile_edges, tile_count, row_group, col_group):
    tile_side = TILE
    col_tiles = col_group // tile_side
    row_tiles = row_group // tile_side
    slot_total = tile_slot.shape[0]
    offsets = jnp.arange(tile_side, dtype=jnp.int32)
    row_onehot = (tile_edges[:, 0, :, None] == offsets[None, None, :]).astype(jnp.bfloat16)
    col_onehot = (tile_edges[:, 1, :, None] == offsets[None, None, :]).astype(jnp.bfloat16)
    slot_tiles = jnp.einsum(
        "ser,sec->src", row_onehot, col_onehot, preferred_element_type=jnp.float32
    )
    slot_tiles = slot_tiles.astype(jnp.bfloat16).reshape(slot_total, tile_side * tile_side)
    slot_live = jnp.arange(slot_total, dtype=jnp.int32) < tile_count
    places = jnp.arange(row_tiles * col_tiles, dtype=jnp.int32)
    place_onehot = ((tile_slot[:, None] == places[None, :]) & slot_live[:, None]).astype(
        jnp.bfloat16
    )
    placed = lax.dot_general(
        place_onehot, slot_tiles, CONTRACT_ROWS, preferred_element_type=jnp.float32
    )
    placed = placed.astype(jnp.bfloat16).reshape(row_tiles, col_tiles, tile_side, tile_side)
    return placed.transpose(0, 2, 1, 3).reshape(row_group, col_group)


def gather_targets(values):
    return lax.all_gather(values, "col", axis=0, tiled=True)


def sum_sources(partial_sums):
    return lax.psum_scatter(partial_sums, "row", scatter_dimension=0, tiled=True)


def per_device(
    features, norm_weight, weight_in, weight_out, labels, tile_slot, tile_edges, tile_count
):
    row_size = lax.axis_size("row")
    col_size = lax.axis_size("col")
    node_rows = features.shape[0]
    total_nodes = node_rows * row_size * col_size
    adjacency = densify(
        tile_slot[0], tile_edges[0], tile_count[0], node_rows * col_size, node_rows * row_size
    )
    node_scale = norm_weight[:, None]
    normed = (node_scale * features.astype(jnp.float32)).astype(jnp.bfloat16)
    source_one = jnp.dot(normed, weight_in, preferred_element_type=jnp.float32)
    gathered_one = lax.all_gather(source_one, "row", axis=0, tiled=True)
    forward_one = jnp.dot(adjacency.astype(jnp.float32), gathered_one, precision=HIGHEST)
    projected = lax.psum_scatter(forward_one, "col", scatter_dimension=0, tiled=True)
    pre_hidden = node_scale * (projected + source_one)
    hidden = jax.nn.relu(pre_hidden).astype(jnp.bfloat16)
    source_two = (
        node_scale * jnp.dot(hidden, weight_out, preferred_element_type=jnp.float32)
    ).astype(jnp.bfloat16)
    gathered_two = lax.all_gather(source_two, "row", axis=0, tiled=True)
    forward_two = jnp.dot(adjacency, gathered_two, preferred_element_type=jnp.float32)
    logits = node_scale * (
        lax.psum_scatter(forward_two, "col", scatter_dimension=0, tiled=True)
        + source_two.astype(jnp.float32)
    )
    capped = SOFTCAP * jnp.tanh(logits / SOFTCAP)
    exp_capped = jnp.exp(capped)
    exp_total = jnp.sum(exp_capped, axis=1, keepdims=True)
    one_hot = (labels[:, None] == jnp.arange(capped.shape[1], dtype=jnp.int32)[None, :]).astype(
        jnp.float32
    )
    loss_local = jnp.sum(jnp.log(exp_total[:, 0]) - jnp.sum(capped * one_hot, axis=1))
    d_logits = (
        LOSS_SCALE
        / total_nodes
        * (exp_capped / exp_total - one_hot)
        * (1.0 - (capped / SOFTCAP) ** 2)
    )
    back_two = (node_scale * d_logits).astype(jnp.bfloat16)
    backward_two = lax.dot_general(
        adjacency, gather_targets(back_two), CONTRACT_ROWS, preferred_element_type=jnp.float32
    )
    d_source_two = node_scale * (sum_sources(backward_two) + back_two.astype(jnp.float32))
    grad_out_local = lax.dot_general(
        hidden.astype(jnp.float32), d_source_two, CONTRACT_ROWS, precision=HIGHEST
    )
    d_hidden = lax.dot_general(
        d_source_two, weight_out.astype(jnp.float32), (((1,), (1,)), ((), ())), precision=HIGHEST
    )
    back_one = (node_scale * jnp.where(pre_hidden > 0, d_hidden, 0.0)).astype(jnp.bfloat16)
    gathered_back = gather_targets(back_one)
    backward_one = lax.dot_general(
        adjacency, gathered_back, CONTRACT_ROWS, preferred_element_type=jnp.float32
    )
    d_source_one = sum_sources(backward_one) + back_one.astype(jnp.float32)
    grad_in_local = lax.dot_general(
        normed.astype(jnp.float32), d_source_one, CONTRACT_ROWS, precision=HIGHEST
    )
    grad_in, grad_out, loss_sum = lax.psum(
        (grad_in_local, grad_out_local, loss_local), ("row", "col")
    )
    return (grad_in, grad_out, loss_sum / total_nodes)


def solution(mesh):
    in_specs = (
        P(("row", "col"), None),
        P(("row", "col")),
        P(),
        P(),
        P(("row", "col")),
        P(("row", "col"), None),
        P(("row", "col"), None, None, None),
        P(("row", "col")),
    )
    out_specs = (P(), P(), P())
    return jax.shard_map(
        per_device, mesh=mesh, in_specs=in_specs, out_specs=out_specs, check_vma=False
    )
```

profile of v0, /device:TPU:0, one launch (start us, length us, event | category | flops | bytes accessed | tf_op | source)
XLA Modules:
  0.0 426.0 jit_solution(7901533714446784060)
XLA Ops:
  7.2 0.0 copy-start
  7.2 0.0 reduce-scatter.5.cloned.1.call-start
  7.2 1.7 fusion.37
  9.0 7.9 %iota_compare_fusion.17 = pred[128,512,128]{1,2,0:T(32,128)(4,1)} fusion(s32[128,512]{1,0:T(8,128)S(1)} %get-tuple-element.10), kind=kLoop, calls=%fused_computation.1.clone.clone.clone.clone.2 | loop fusion | flops 8388608 | bytes 8650752 | tf_op jit(solution)/shard_map/ser,sec->src/dot_general | solution.py:21
  17.6 0.0 copy-start.6
  17.6 14.4 %fusion.5 = bf16[128,128,128]{2,1,0:T(8,128)(2,1)S(1)} fusion(s32[128,512]{1,0:T(8,128)S(1)} %get-tuple-element.9, pred[128,512,128]{1,2,0:T(32,128)(4,1)} %iota_compare_fusion.17), kind=kOutput, calls=%fused_computation.8 | convolution fusion | flops 2157969408 | bytes 12845056 | tf_op jit(solution)/shard_map/ser,sec->src/dot_general | solution.py:21
  32.0 0.0 copy-start.4
  32.0 0.0 copy-start.2
  32.0 0.0 copy-start.3
  32.1 0.0 copy-done.6
  32.1 0.0 copy-start.5
  32.1 2.6 fusion.6
  34.7 0.2 copy.23
  34.9 0.7 copy.15
  35.6 0.0 copy-done.4
  35.7 0.1 copy.14
  35.8 0.0 copy-done.2
  35.8 0.0 copy-done.3
  35.8 0.2 fusion.34
  36.0 8.6 %all_gather.12 = f32[512,256]{1,0:T(8,128)S(1)} all-gather(f32[128,256]{1,0:T(8,128)S(1)} %fusion.34), channel_id=1, replica_groups=mesh['row'=4,'col'=8] {'row'}, dimensions={0}, use_global_device_ids=true | all-gather | bytes 655360 | tf_op jit(solution)/shard_map/all_gather | solution.py:58
  44.6 2.2 fusion.18
  46.8 0.0 reduce-scatter.5.cloned.1.call-update
  46.9 0.0 reduce-scatter.7.cloned.1.call-start
  46.9 64.4 %reduce-scatter.5.cloned.1.call-done = f32[128,256]{1,0:T(8,128)} async-done(((f32[1024,256]{1,0:T(8,128)}), f32[128,256]{1,0:T(8,128)}) %reduce-scatter.5.cloned.1.call-update) | async-done | bytes 131088 | tf_op jit(solution)/shard_map/reduce_scatter | solution.py:60
  111.3 0.0 copy-done
  111.3 0.0 copy-start.1
  111.3 1.2 fusion.11
  112.6 5.4 %all_gather.13 = bf16[512,128]{0,1:T(8,128)(2,1)S(1)} all-gather(bf16[128,128]{0,1:T(8,128)(2,1)S(1)} %fusion.11), channel_id=1, replica_groups=mesh['row'=4,'col'=8] {'row'}, dimensions={0}, use_global_device_ids=true | all-gather | bytes 163840 | tf_op jit(solution)/shard_map/all_gather | solution.py:66
  118.0 1.1 fusion.16
  119.1 0.0 reduce-scatter.7.cloned.1.call-update
  119.1 0.0 reduce-scatter.9.cloned.1.call-start
  119.2 61.5 %reduce-scatter.7.cloned.1.call-done = f32[128,128]{0,1:T(8,128)} async-done(((f32[1024,128]{0,1:T(8,128)}), f32[128,128]{0,1:T(8,128)}) %reduce-scatter.7.cloned.1.call-update) | async-done | bytes 65552 | tf_op jit(solution)/shard_map/reduce_scatter | solution.py:69
  180.7 0.0 copy-done.5
  180.7 0.9 select_reduce_fusion
  181.6 0.9 multiply_convert_fusion
  182.5 26.7 %all_gather.14 = bf16[1024,128]{0,1:T(8,128)(2,1)S(1)} all-gather(bf16[128,128]{0,1:T(8,128)(2,1)S(1)} %multiply_convert_fusion), channel_id=1, replica_groups=mesh['row'=4,'col'=8] {'col'}, dimensions={0}, use_global_device_ids=true | all-gather | bytes 294912 | tf_op jit(solution)/shard_map/all_gather | solution.py:38
  209.2 1.2 fusion.14
  210.3 0.0 reduce-scatter.9.cloned.1.call-update
  210.4 0.0 reduce-scatter.11.cloned.1.call-start
  210.4 17.7 %reduce-scatter.9.cloned.1.call-done = f32[128,128]{0,1:T(8,128)} async-done(((f32[512,128]{0,1:T(8,128)}), f32[128,128]{0,1:T(8,128)}) %reduce-scatter.9.cloned.1.call-update) | async-done | bytes 65552 | tf_op jit(solution)/shard_map/reduce_scatter | solution.py:42
  228.1 1.2 fusion.10
  229.3 31.4 %all_gather.15 = bf16[1024,256]{1,0:T(8,128)(2,1)S(1)} all-gather(bf16[128,256]{1,0:T(8,128)(2,1)S(1)} %fusion.10), channel_id=1, replica_groups=mesh['row'=4,'col'=8] {'col'}, dimensions={0}, use_global_device_ids=true | all-gather | bytes 589824 | tf_op jit(solution)/shard_map/all_gather | solution.py:38
  260.7 1.2 fusion.12
  262.0 0.0 reduce-scatter.11.cloned.1.call-update
  262.0 0.0 all-reduce.3.cloned.1.call-start
  262.0 0.0 copy-done.1
  262.0 1.8 fusion.29
  263.9 20.0 %reduce-scatter.11.cloned.1.call-done = f32[128,256]{1,0:T(8,128)} async-done(((f32[512,256]{1,0:T(8,128)}), f32[128,256]{1,0:T(8,128)}) %reduce-scatter.11.cloned.1.call-update) | async-done | bytes 131088 | tf_op jit(solution)/shard_map/reduce_scatter | solution.py:42
  283.8 1.8 fusion.24
  285.6 0.0 all-reduce.3.cloned.1.call-update
  285.7 0.6 subtract_reduce_fusion
  286.3 39.5 %psum.23 = f32[]{:T(128)} all-reduce(f32[]{:T(128)} %subtract_reduce_fusion), channel_id=1, replica_groups=mesh['row'=4,'col'=8] {'row','col'}, use_global_device_ids=true, to_apply=%region_9.10 | all-reduce | flops 1 | bytes 8 | tf_op jit(solution)/shard_map/psum | solution.py:105
  326.5 88.7 %all-reduce.3.cloned.1.call-done = (f32[128,256]{1,0:T(8,128)}, f32[256,128]{1,0:T(8,128)}) async-done(((f32[128,256]{1,0:T(8,128)}, f32[256,128]{1,0:T(8,128)}), (f32[128,256]{1,0:T(8,128)}, f32[256,128]{1,0:T(8,128)})) %all-reduce.3.cloned.1.call-update) | async-done | bytes 262160 | tf_op jit(solution)/shard_map/psum | solution.py:105
  415.2 1.6 copy.54
  416.7 1.6 copy.55
  (2 shorter events, 0.0 us)
Async XLA Ops:
  7.2 104.2 %copy-start = (bf16[256,128]{1,0:T(8,128)(2,1)S(1)}, bf16[256,128]{1,0:T(8,128)(2,1)}, u32[]{:S(2)}) copy-start(bf16[256,128]{1,0:T(8,128)(2,1)} %param.11) | copy-start | bytes 196612
  7.2 104.1 %reduce-scatter.5.cloned.1.call-start = ((), (), s32[]{:S(2)}) async-start(), calls=%async_computation.4 | async-start | bytes 1179648 | tf_op jit(solution)/shard_map/reduce_scatter | solution.py:60
  17.6 14.5 %copy-start.6 = (s32[1,128]{1,0:T(1,128)S(1)}, s32[1,128]{1,0:T(1,128)}, u32[]{:S(2)}) copy-start(s32[1,128]{1,0:T(1,128)} %param.13) | copy-start | bytes 1540
  32.0 3.6 copy-start.4
  32.0 3.7 copy-start.2
  32.0 3.7 copy-start.3
  32.1 148.6 %copy-start.5 = (s32[128]{0:T(128)S(1)}, s32[128]{0:T(128)}, u32[]{:S(2)}) copy-start(s32[128]{0:T(128)} %param.12) | copy-start | bytes 1540
  46.9 133.8 %reduce-scatter.7.cloned.1.call-start = ((), (), s32[]{:S(2)}) async-start(), calls=%async_computation.5 | async-start | bytes 589824 | tf_op jit(solution)/shard_map/reduce_scatter | solution.py:69
  111.3 150.7 %copy-start.1 = (f32[128,256]{1,0:T(8,128)S(1)}, f32[128,256]{1,0:T(8,128)}, u32[]{:S(2)}) copy-start(f32[128,256]{1,0:T(8,128)} %reduce-scatter.5.cloned.1.call-done) | copy-start | bytes 393220
  119.1 109.0 %reduce-scatter.9.cloned.1.call-start = ((), (), s32[]{:S(2)}) async-start(), calls=%async_computation.6 | async-start | bytes 327680 | tf_op jit(solution)/shard_map/reduce_scatter | solution.py:42
  210.4 73.5 %reduce-scatter.11.cloned.1.call-start = ((), (), s32[]{:S(2)}) async-start(), calls=%async_computation.7 | async-start | bytes 655360 | tf_op jit(solution)/shard_map/reduce_scatter | solution.py:42
  262.0 153.2 %all-reduce.3.cloned.1.call-start = ((), (), s32[]{:S(2)}) async-start(), calls=%async_computation.8 | async-start | bytes 524288 | tf_op jit(solution)/shard_map/psum | solution.py:105
Sparse Core Ops, SparseCore 0:
  47.0 64.3 reduce-scatter.4
  119.2 61.4 reduce-scatter.6
  210.5 17.5 reduce-scatter.8
  262.1 21.6 reduce-scatter.10
  289.9 125.1 all-reduce.2
where the time goes:
time: 426 us
  waiting for transfers between devices  252 us (59%)
  blocking collectives  112 us (26%)
  matrix products  29 us (7%)
  between operations  16.4 us (4%)
  other arithmetic  10.3 us (2%)
  local copies, waits for them, and re-layouts  6.02 us (1%)
    psum x1, waiting for transfers between devices, per_device(): lax.psum((grad_in_local, grad_out_local, loss_local), ('row', 'col'))  88.7 us
    reduce_scatter x1, waiting for transfers between devices, per_device(): lax.psum_scatter(forward_one, 'col', scatter_dimension=0, tiled=True)  64.4 us
    reduce_scatter x1, waiting for transfers between devices, per_device(): lax.psum_scatter(forward_two, 'col', scatter_dimension=0, tiled=True)  61.5 us
    all_gather x2, blocking collectives, gather_targets(): return lax.all_gather(values, 'col', axis=0, tiled=True)  58.1 us
    psum x1, blocking collectives, per_device(): lax.psum((grad_in_local, grad_out_local, loss_local), ('row', 'col'))  39.5 us
    reduce_scatter x2, waiting for transfers between devices, sum_sources(): lax.psum_scatter(partial_sums, 'row', scatter_dimension=0, tiled=True)  37.7 us
    dot_general x1, matrix products, densify(): jnp.einsum('ser,sec->src', row_onehot, col_onehot, preferred_element_type...  14.4 us
    all_gather x1, blocking collectives, per_device(): gathered_one = lax.all_gather(source_one, 'row', axis=0, tiled=True)  8.65 us
  transfers between devices with their start and end apart: 5, of which 5 were waited for; matrix products, arithmetic and copies ran while one was open for 1% of the time, Pallas kernels for 0%

commit v1 on v0

--- a/solution.py
+++ b/solution.py
@@ -55,7 +55,11 @@
     node_scale = norm_weight[:, None]
     normed = (node_scale * features.astype(jnp.float32)).astype(jnp.bfloat16)
     source_one = jnp.dot(normed, weight_in, preferred_element_type=jnp.float32)
-    gathered_one = lax.all_gather(source_one, "row", axis=0, tiled=True)
+    num = lax.psum(1, axis_name="row")
+    blocks_here = [num if pp == 0 else 1 for pp in range(source_one.ndim)]
+    gathered_one = lax.all_to_all(
+        jnp.tile(source_one, blocks_here), "row", split_axis=0, concat_axis=0, tiled=True
+    )
     forward_one = jnp.dot(adjacency.astype(jnp.float32), gathered_one, precision=HIGHEST)
     projected = lax.psum_scatter(forward_one, "col", scatter_dimension=0, tiled=True)
     pre_hidden = node_scale * (projected + source_one)

time: 426 us -> 426 us (level)
  blocking collectives: 112 us -> 103 us
    all_gather x1 -> x0, blocking collectives: 8.65 us -> none  [per_device(): gathered_one = lax.all_gather(source_one, 'row', axis=0, tiled=True)]
  transfers between devices with their start and end apart: 5 -> 6, of which waited for: 5 -> 5; matrix products, arithmetic and copies ran while one was open for 1% -> 7% of each run, Pallas kernels for 0% -> 0%
where the time goes in v1:
time: 426 us
  waiting for transfers between devices  254 us (60%)
  blocking collectives  103 us (24%)
  matrix products  29.8 us (7%)
  between operations  16.3 us (4%)
  other arithmetic  10.3 us (2%)
  local copies, waits for them, and re-layouts  7.68 us (2%)
  starting transfers between devices  4.41 us (1%)
    psum x1, waiting for transfers between devices, per_device(): lax.psum((grad_in_local, grad_out_local, loss_local), ('row', 'col'))  88.8 us
    reduce_scatter x1, waiting for transfers between devices, per_device(): lax.psum_scatter(forward_one, 'col', scatter_dimension=0, tiled=True)  66 us
    reduce_scatter x1, waiting for transfers between devices, per_device(): lax.psum_scatter(forward_two, 'col', scatter_dimension=0, tiled=True)  61.5 us
    all_gather x2, blocking collectives, gather_targets(): return lax.all_gather(values, 'col', axis=0, tiled=True)  58 us
    psum x1, blocking collectives, per_device(): lax.psum((grad_in_local, grad_out_local, loss_local), ('row', 'col'))  39.5 us
    reduce_scatter x2, waiting for transfers between devices, sum_sources(): lax.psum_scatter(partial_sums, 'row', scatter_dimension=0, tiled=True)  37.7 us
    dot_general x1, matrix products, densify(): jnp.einsum('ser,sec->src', row_onehot, col_onehot, preferred_element_type...  14.4 us
  transfers between devices with their start and end apart: 6, of which 5 were waited for; matrix products, arithmetic and copies ran while one was open for 7% of the time, Pallas kernels for 0%

profile of v1, /device:TPU:0, one launch (start us, length us, event | category | flops | bytes accessed | tf_op | source)
XLA Modules:
  0.0 425.6 jit_solution(10749664166264035728)
XLA Ops:
  7.2 0.0 copy-start
  7.2 0.9 copy.14
  8.1 1.1 fusion.34
  9.1 0.9 tile.2
  10.0 4.2 all-to-all-start
  14.3 0.0 reduce-scatter.5.cloned.1.call-start
  14.3 1.7 fusion.37
  16.1 7.9 %iota_compare_fusion.17 = pred[128,512,128]{1,2,0:T(32,128)(4,1)} fusion(s32[128,512]{1,0:T(8,128)S(1)} %get-tuple-element.10), kind=kLoop, calls=%fused_computation.1.clone.clone.clone.clone.2 | loop fusion | flops 8388608 | bytes 8650752 | tf_op jit(solution)/shard_map/ser,sec->src/dot_general | solution.py:21
  24.6 0.0 copy-start.4
  24.6 14.4 %fusion.5 = bf16[128,128,128]{2,1,0:T(8,128)(2,1)S(1)} fusion(s32[128,512]{1,0:T(8,128)S(1)} %get-tuple-element.9, pred[128,512,128]{1,2,0:T(32,128)(4,1)} %iota_compare_fusion.17), kind=kOutput, calls=%fused_computation.8 | convolution fusion | flops 2157969408 | bytes 12845056 | tf_op jit(solution)/shard_map/ser,sec->src/dot_general | solution.py:21
  39.1 0.0 copy-start.2
  39.1 0.0 copy-start.3
  39.1 0.0 copy-done.4
  39.1 2.6 fusion.6
  41.7 0.2 copy.23
  41.9 0.7 copy.15
  42.7 0.0 all-to-all-done
  42.7 2.2 fusion.18
  44.9 0.0 reduce-scatter.5.cloned.1.call-update
  44.9 0.0 reduce-scatter.7.cloned.1.call-start
  44.9 66.0 %reduce-scatter.5.cloned.1.call-done = f32[128,256]{1,0:T(8,128)} async-done(((f32[1024,256]{1,0:T(8,128)}), f32[128,256]{1,0:T(8,128)}) %reduce-scatter.5.cloned.1.call-update) | async-done | bytes 131088 | tf_op jit(solution)/shard_map/reduce_scatter | solution.py:64
  110.9 0.0 copy-done
  110.9 0.0 copy-done.2
  110.9 0.0 copy-start.1
  110.9 1.2 fusion.11
  112.1 5.4 %all_gather.9 = bf16[512,128]{0,1:T(8,128)(2,1)S(1)} all-gather(bf16[128,128]{0,1:T(8,128)(2,1)S(1)} %fusion.11), channel_id=1, replica_groups=mesh['row'=4,'col'=8] {'row'}, dimensions={0}, use_global_device_ids=true | all-gather | bytes 163840 | tf_op jit(solution)/shard_map/all_gather | solution.py:70
  117.6 1.1 fusion.16
  118.7 0.0 reduce-scatter.7.cloned.1.call-update
  118.7 0.0 reduce-scatter.9.cloned.1.call-start
  118.8 61.5 %reduce-scatter.7.cloned.1.call-done = f32[128,128]{0,1:T(8,128)} async-done(((f32[1024,128]{0,1:T(8,128)}), f32[128,128]{0,1:T(8,128)}) %reduce-scatter.7.cloned.1.call-update) | async-done | bytes 65552 | tf_op jit(solution)/shard_map/reduce_scatter | solution.py:73
  180.3 0.0 copy-done.3
  180.3 0.9 select_reduce_fusion
  181.2 0.9 multiply_convert_fusion
  182.1 26.6 %all_gather.10 = bf16[1024,128]{0,1:T(8,128)(2,1)S(1)} all-gather(bf16[128,128]{0,1:T(8,128)(2,1)S(1)} %multiply_convert_fusion), channel_id=1, replica_groups=mesh['row'=4,'col'=8] {'col'}, dimensions={0}, use_global_device_ids=true | all-gather | bytes 294912 | tf_op jit(solution)/shard_map/all_gather | solution.py:38
  208.7 1.2 fusion.14
  209.9 0.0 reduce-scatter.9.cloned.1.call-update
  209.9 0.0 reduce-scatter.11.cloned.1.call-start
  210.0 17.7 %reduce-scatter.9.cloned.1.call-done = f32[128,128]{0,1:T(8,128)} async-done(((f32[512,128]{0,1:T(8,128)}), f32[128,128]{0,1:T(8,128)}) %reduce-scatter.9.cloned.1.call-update) | async-done | bytes 65552 | tf_op jit(solution)/shard_map/reduce_scatter | solution.py:42
  227.7 1.2 fusion.10
  228.9 31.4 %all_gather.11 = bf16[1024,256]{1,0:T(8,128)(2,1)S(1)} all-gather(bf16[128,256]{1,0:T(8,128)(2,1)S(1)} %fusion.10), channel_id=1, replica_groups=mesh['row'=4,'col'=8] {'col'}, dimensions={0}, use_global_device_ids=true | all-gather | bytes 589824 | tf_op jit(solution)/shard_map/all_gather | solution.py:38
  260.3 1.2 fusion.12
  261.5 0.0 reduce-scatter.11.cloned.1.call-update
  261.6 0.0 all-reduce.3.cloned.1.call-start
  261.6 0.0 copy-done.1
  261.6 1.8 fusion.29
  263.4 20.0 %reduce-scatter.11.cloned.1.call-done = f32[128,256]{1,0:T(8,128)} async-done(((f32[512,256]{1,0:T(8,128)}), f32[128,256]{1,0:T(8,128)}) %reduce-scatter.11.cloned.1.call-update) | async-done | bytes 131088 | tf_op jit(solution)/shard_map/reduce_scatter | solution.py:42
  283.4 1.8 fusion.24
  285.2 0.0 all-reduce.3.cloned.1.call-update
  285.2 0.6 subtract_reduce_fusion
  285.8 39.5 %psum.23 = f32[]{:T(128)} all-reduce(f32[]{:T(128)} %subtract_reduce_fusion), channel_id=1, replica_groups=mesh['row'=4,'col'=8] {'row','col'}, use_global_device_ids=true, to_apply=%region_9.10 | all-reduce | flops 1 | bytes 8 | tf_op jit(solution)/shard_map/psum | solution.py:109
  326.0 88.8 %all-reduce.3.cloned.1.call-done = (f32[128,256]{1,0:T(8,128)}, f32[256,128]{1,0:T(8,128)}) async-done(((f32[128,256]{1,0:T(8,128)}, f32[256,128]{1,0:T(8,128)}), (f32[128,256]{1,0:T(8,128)}, f32[256,128]{1,0:T(8,128)})) %all-reduce.3.cloned.1.call-update) | async-done | bytes 262160 | tf_op jit(solution)/shard_map/psum | solution.py:109
  414.8 1.6 copy.54
  416.4 1.6 copy.55
  (2 shorter events, 0.0 us)
Async XLA Ops:
  7.2 103.7 %copy-start = (bf16[256,128]{1,0:T(8,128)(2,1)S(1)}, bf16[256,128]{1,0:T(8,128)(2,1)}, u32[]{:S(2)}) copy-start(bf16[256,128]{1,0:T(8,128)(2,1)} %param.11) | copy-start | bytes 196612
  10.0 32.6 %all-to-all-start = ((f32[4,128,256]{2,1,0:T(8,128)}), f32[4,128,256]{2,1,0:T(8,128)S(1)}, u32[]{:S(2)}, u32[]{:S(2)}) async-start(f32[4,128,256]{2,1,0:T(8,128)} %tile.2), calls=%async_computation | async-start | bytes 1048576 | tf_op jit(solution)/shard_map/all_to_all | solution.py:60
  14.3 96.6 %reduce-scatter.5.cloned.1.call-start = ((), (), s32[]{:S(2)}) async-start(), calls=%async_computation.5 | async-start | bytes 1179648 | tf_op jit(solution)/shard_map/reduce_scatter | solution.py:64
  24.6 14.5 %copy-start.4 = (s32[1,128]{1,0:T(1,128)S(1)}, s32[1,128]{1,0:T(1,128)}, u32[]{:S(2)}) copy-start(s32[1,128]{1,0:T(1,128)} %param.13) | copy-start | bytes 1540
  39.1 71.9 %copy-start.2 = (f32[128]{0:T(128)S(1)}, f32[128]{0:T(128)}, u32[]{:S(2)}) copy-start(f32[128]{0:T(128)} %param.9) | copy-start | bytes 1540
  39.1 141.2 %copy-start.3 = (s32[128]{0:T(128)S(1)}, s32[128]{0:T(128)}, u32[]{:S(2)}) copy-start(s32[128]{0:T(128)} %param.12) | copy-start | bytes 1540
  44.9 135.4 %reduce-scatter.7.cloned.1.call-start = ((), (), s32[]{:S(2)}) async-start(), calls=%async_computation.6 | async-start | bytes 589824 | tf_op jit(solution)/shard_map/reduce_scatter | solution.py:73
  110.9 150.7 %copy-start.1 = (f32[128,256]{1,0:T(8,128)S(1)}, f32[128,256]{1,0:T(8,128)}, u32[]{:S(2)}) copy-start(f32[128,256]{1,0:T(8,128)} %reduce-scatter.5.cloned.1.call-done) | copy-start | bytes 393220
  118.7 109.0 %reduce-scatter.9.cloned.1.call-start = ((), (), s32[]{:S(2)}) async-start(), calls=%async_computation.7 | async-start | bytes 327680 | tf_op jit(solution)/shard_map/reduce_scatter | solution.py:42
  209.9 73.5 %reduce-scatter.11.cloned.1.call-start = ((), (), s32[]{:S(2)}) async-start(), calls=%async_computation.8 | async-start | bytes 655360 | tf_op jit(solution)/shard_map/reduce_scatter | solution.py:42
  261.6 153.2 %all-reduce.3.cloned.1.call-start = ((), (), s32[]{:S(2)}) async-start(), calls=%async_computation.9 | async-start | bytes 524288 | tf_op jit(solution)/shard_map/psum | solution.py:109
Sparse Core Ops, SparseCore 0:
  45.0 65.8 reduce-scatter.4
  118.8 61.4 reduce-scatter.6
  210.0 17.6 reduce-scatter.8
  261.7 21.6 reduce-scatter.10
  289.5 125.2 all-reduce.2
